TPU v7x, 128 devices: a whole 4x4x4 slice. The times are simulated.
128 devices in a mesh: box: 8 (over z, core), dir: 16 (over x, y).
Axes of the slice: x: 4, y: 4, z: 4, core: 2. Of those that a mesh axis runs over, the one named last changes fastest.
Arguments:
- currents: bfloat16 [16384, 256, 128], P(('box', 'dir')), may hold values from -6 to 6
- leaf_parent: int32 [16384], P(('box', 'dir')), may hold values from 0 to 255, as said below
- near_links: int32 [16384, 2], P(('box', 'dir')), may hold values 0 or 1
- near_blocks: bfloat16 [3, 256, 256], replicated, may hold values from -0.375 to 0.375
- aggregate_maps: bfloat16 [64, 256, 256], replicated, may hold values from -0.375 to 0.375
- far_boxes: int32 [256, 64], P('box'), may hold values from 0 to 255
- far_counts: int32 [256], P('box'), may hold values from 16 to 64
- translate_coef: float32 [256, 64, 256], P('box'), may hold values from 0.005 to 0.05
- time_kernel: float32 [128], replicated, may hold values from -0.5 to 0.5
- disaggregate_maps: bfloat16 [64, 256, 256], replicated, may hold values from -0.375 to 0.375
Outputs:
- field: bfloat16 [16384, 256, 128], P(('box', 'dir'))
Inputs may be any that keep to these rules, and one draw needn't show every extreme that they name: `leaf_parent`: the leaves k * 64 to (k + 1) * 64 - 1 share one parent. The leaves g * 2048 to (g + 1) * 2048 - 1 have as parents the top-level boxes g * 32 to (g + 1) * 32 - 1, each exactly once as a run.
All inputs are finite; a program needn't handle non-finite values. No bound on the sum of `near_links` on one device may be relied on, other than what follows from the above.
Results may differ from a plain program's by a relative error of at most 0.0047.
Values may be sent and summed in bfloat16 or wider, within the bound.
No kernel may reach another device: no remote copies, remote signals or barrier semaphores. Data moves between devices by JAX's collectives and lax.ppermute only.
A program may use at most 192 MiB of HBM per device.

v0:
```python
import jax
import jax.numpy as jnp
from jax import lax
from jax.sharding import Mesh
from jax.sharding import PartitionSpec as P

LEAF_TOP = 64
BOX = ("box_0", "box_1")
BOX_DIR = ("box_0", "box_1", "dir")


def in_blocks(array, dim, devices):
    before, after = (array.shape[:dim], array.shape[dim + 1 :])
    return jnp.moveaxis(array.reshape(*before, devices, -1, *after), dim, 0)


def summed_on_arrival(array, axis, dim):
    tiles = in_blocks(array, dim, lax.axis_size(axis))
    arrived = lax.all_to_all(tiles, axis, split_axis=0, concat_axis=0, tiled=True)
    return arrived.sum(axis=0)


def edges_of(length, count):
    unit = 8 if length >= 8 * count else 1
    return [length // unit * k // count * unit for k in range(1, count)]


def all_blocks(array, axes, sequence):
    tiles = array[None]
    for k in sequence:
        tiles = lax.all_gather(tiles, axes[k], axis=0, tiled=True)
    held = [lax.axis_size(axes[k]) for k in reversed(sequence)]
    tiles = tiles.reshape(*held, *array.shape)
    turned = sorted(range(len(sequence)), key=lambda place: sequence[len(sequence) - 1 - place])
    return tiles.transpose(*turned, *range(len(sequence), tiles.ndim)).reshape(-1, *array.shape)


def in_order(tiles, dim):
    shape = list(tiles.shape[1:])
    shape[dim] *= tiles.shape[0]
    return jnp.moveaxis(tiles, 0, dim).reshape(shape)


def spread_gather(array, axes, dim):
    numbers = list(range(len(axes)))[::-1]
    cut = array.shape.index(max(array.shape[:-1] or array.shape))
    edges = [0, *edges_of(array.shape[cut], len(axes)), array.shape[cut]]
    done = []
    for k, (start, end) in enumerate(zip(edges, edges[1:])):
        if end > start:
            share = lax.slice_in_dim(array, start, end, axis=cut)
            done.append(all_blocks(share, axes, numbers[k:] + numbers[:k]))
    return in_order(jnp.concatenate(done, axis=cut + 1), dim)


def sent_to_all(array, axis):
    devices = lax.axis_size(axis)
    return lax.all_to_all(
        jnp.broadcast_to(array[None], (devices, *array.shape)), axis, 0, 0, tiled=True
    )


def collect(array, axis, dim):
    return in_order(sent_to_all(array, axis), dim)


def with_halo(block, sides, width):
    for axis, dim in sides:
        count = lax.axis_size(axis)
        forward = [(i, i + 1) for i in range(count - 1)]
        backward = [(target, source) for source, target in forward]
        low = lax.ppermute(
            lax.slice_in_dim(block, block.shape[dim] - width, None, axis=dim), axis, forward
        )
        high = lax.ppermute(lax.slice_in_dim(block, 0, width, axis=dim), axis, backward)
        block = jnp.concatenate([low, block, high], axis=dim)
    return block


def time_matrix(kernel):
    length = kernel.shape[0]
    sample_lag = jnp.arange(length)[:, None] - jnp.arange(length)[None, :]
    return jnp.where(
        sample_lag >= 0, kernel[jnp.clip(sample_lag, 0, length - 1)], jnp.zeros((), kernel.dtype)
    )


def per_device(
    currents,
    leaf_parent,
    near_links,
    near_blocks,
    aggregate_maps,
    far_boxes,
    far_counts,
    translate_coef,
    time_kernel,
    disaggregate_maps,
):
    highest = lax.Precision.HIGHEST
    leaf_count, unknowns, samples = currents.shape
    run_length = min(leaf_count, LEAF_TOP)
    run_count = leaf_count // run_length
    top_local, list_slots = far_boxes.shape
    top_total = top_local * lax.axis_size(BOX)
    direction_total = aggregate_maps.shape[1]
    dir_rows = direction_total // lax.axis_size("dir")
    dir_index = lax.axis_index("dir")
    local_parent = leaf_parent - lax.axis_index(BOX) * top_local
    run_parent = local_parent.reshape(run_count, run_length)[:, 0]
    run_onehot = (run_parent[:, None] == jnp.arange(top_local)[None, :]).astype(jnp.float32)
    leaf_runs = currents.reshape(run_count, run_length, unknowns, samples)
    map_block = aggregate_maps
    run_sums = jnp.einsum("sqp,bspt->bqt", map_block, leaf_runs, preferred_element_type=jnp.float32)
    own_rays = summed_on_arrival(
        jnp.einsum("bc,bqt->qct", run_onehot, run_sums, precision=highest), "dir", 0
    )
    own_rays = own_rays.astype(jnp.bfloat16)
    is_valid = (jnp.arange(list_slots)[None, :] < far_counts[:, None]).astype(jnp.float32)
    matches = (far_boxes[:, :, None] == jnp.arange(top_total)[None, None, :]).astype(
        jnp.float32
    ) * is_valid[:, :, None]
    coef_block = lax.dynamic_slice_in_dim(translate_coef, dir_index * dir_rows, dir_rows, 2)
    weights = jnp.einsum("cfs,cfq->csq", matches, coef_block, precision=highest)
    far_sum = jnp.einsum(
        "csq,qst->cqt",
        weights,
        spread_gather(own_rays, BOX, 1).astype(jnp.float32),
        precision=highest,
    )
    incoming = jnp.einsum(
        "cqs,ts->cqt", far_sum, time_matrix(time_kernel), precision=highest
    ).astype(jnp.bfloat16)
    selected = jnp.einsum(
        "bc,cqt->bqt",
        run_onehot,
        collect(incoming, "dir", 1).astype(jnp.float32),
        precision=highest,
    ).astype(jnp.bfloat16)
    map_block = disaggregate_maps
    far_terms = jnp.einsum("spq,bqt->bspt", map_block, selected, preferred_element_type=jnp.float32)
    far_field = far_terms.reshape(leaf_count, unknowns, samples)
    rim_leaves = jnp.concatenate([currents[:1], currents[-1:]], axis=0)
    extended = with_halo(rim_leaves, ((BOX_DIR, 0),), 1)
    link_mask = near_links.astype(jnp.float32)
    self_term = jnp.einsum(
        "pr,lrt->lpt", near_blocks[0], currents, preferred_element_type=jnp.float32
    )
    before_all = jnp.einsum(
        "pr,lrt->lpt", near_blocks[1], currents, preferred_element_type=jnp.float32
    )
    after_all = jnp.einsum(
        "pr,lrt->lpt", near_blocks[2], currents, preferred_element_type=jnp.float32
    )
    before_rim = jnp.dot(near_blocks[1], extended[0], preferred_element_type=jnp.float32)
    after_rim = jnp.dot(near_blocks[2], extended[3], preferred_element_type=jnp.float32)
    before_term = jnp.concatenate([before_rim[None], before_all[:-1]], axis=0)
    after_term = jnp.concatenate([after_all[1:], after_rim[None]], axis=0)
    near_field = (
        self_term
        + link_mask[:, 0, None, None] * before_term
        + link_mask[:, 1, None, None] * after_term
    )
    return (near_field + far_field).astype(jnp.bfloat16)


def solution(mesh):
    finer = Mesh(mesh.devices.reshape(4, 2, mesh.shape["dir"]), ("box_0", "box_1", "dir"))
    in_specs = (
        P(BOX_DIR, None, None),
        P(BOX_DIR),
        P(BOX_DIR, None),
        P(),
        P(),
        P(BOX, None),
        P(BOX),
        P(BOX, None, None),
        P(),
        P(),
    )
    out_specs = P(BOX_DIR, None, None)
    return jax.shard_map(
        per_device, mesh=finer, in_specs=in_specs, out_specs=out_specs, check_vma=False
    )
```

profile of v0, /device:TPU:34, one launch (start us, length us, event | category | flops | bytes accessed | tf_op | source)
XLA Modules:
  0.0 256.3 jit_solution(14275734861325544151)
XLA Ops:
  0.0 8.3 %fusion.12 = f32[2,256,128]{1,2,0:T(8,128)S(1)} fusion(bf16[2,64,256,128]{3,2,1,0:T(8,128)(2,1)} %bitcast.96, bf16[64,256,256]{2,1,0:T(8,128)(2,1)} %param.14), kind=kOutput, calls=%fused_computation.18 | convolution fusion | flops 2147483648 | bytes 17039360 | tf_op jit(solution)/shard_map/sqp,bspt->bqt/dot_general | solution.py:114
  8.7 3.9 %fusion.47 = f32[256,128,32]{1,2,0:T(8,128)} fusion(f32[2,256,128]{2,0,1:T(2,128)S(1)} %copy.60, s32[2]{0:T(128)S(1)} %slice_reduce_fusion), kind=kOutput, calls=%fused_computation.56 | convolution fusion | flops 25165888 | bytes 4456456 | tf_op jit(solution)/shard_map/bc,bqt->qct/dot_general | solution.py:116
  12.7 7.5 %all-to-all-start = ((f32[16,16,32,128]{3,2,1,0:T(8,128)}), f32[16,16,32,128]{3,2,1,0:T(8,128)}, u32[]{:S(2)}, u32[]{:S(2)}) async-start(f32[16,16,32,128]{3,2,1,0:T(8,128)} %bitcast.97), calls=%async_computation | async-start | bytes 8388608 | tf_op jit(solution)/shard_map/all_to_all | solution.py:19
  20.1 0.9 fusion.55
  21.0 3.4 %collective-permute-start = (bf16[1,256,128]{2,1,0:T(8,128)(2,1)S(1)}, bf16[1,256,128]{2,1,0:T(8,128)(2,1)S(1)}, u32[]{:S(2)}, u32[]{:S(2)}) collective-permute-start(bf16[1,256,128]{2,1,0:T(8,128)(2,1)S(1)} %get-tuple-element.6), channel_id=1, source_target_pairs={{0,1},{1,2},{2,3},{3,4},{4,5},{5,6},{6,7},{7,8},{8,9},{9,10},{10,1... | collective-permute-start | bytes 196616 | tf_op jit(solution)/shard_map/ppermute | solution.py:72
  24.4 4.6 %collective-permute-start.1 = (bf16[1,256,128]{2,1,0:T(8,128)(2,1)S(1)}, bf16[1,256,128]{2,1,0:T(8,128)(2,1)S(1)}, u32[]{:S(2)}, u32[]{:S(2)}) collective-permute-start(bf16[1,256,128]{2,1,0:T(8,128)(2,1)S(1)} %get-tuple-element.5), channel_id=1, source_target_pairs={{1,0},{2,1},{3,2},{4,3},{5,4},{6,5},{7,6},{8,7},{9,8},{10,9},{11,1... | collective-permute-start | bytes 196616 | tf_op jit(solution)/shard_map/ppermute | solution.py:75
  29.1 97.2 %gather_fusion = f32[16384]{0:T(1024)S(1)} fusion(f32[128]{0:T(128)S(1)} %copy-done.2, s32[16384]{0:T(1024)S(1)} %fusion.39), kind=kCustom, calls=%fused_computation | custom fusion | bytes 196608 | tf_op jit(solution)/shard_map/gather | solution.py:84
  126.4 2.9 %fusion.10 = f32[32,256,16]{1,2,0:T(8,128)S(1)} fusion(f32[32,64,256]{2,1,0:T(8,128)S(1)} %copy-done, s32[]{:T(128)S(6)} %select_n.17, f32[32,64]{1,0:T(8,128)S(1)} %fusion.45, s32[32,64]{1,0:T(8,128)S(1)} %copy-done.6), kind=kOutput, calls=%fused_computation.15 | convolution fusion | flops 101711872 | bytes 1605636 | tf_op jit(solution)/shard_map/cfs,cfq->csq/dot_general | solution.py:124
  129.3 2.6 %reduce_sum.9 = bf16[16,32,128]{2,1,0:T(8,128)(2,1)S(1)} reduce(f32[16,16,32,128]{3,2,1,0:T(8,128)} %all-to-all-done, f32[]{:T(128)} %constant.11.clone.1), dimensions={0}, to_apply=%region_0.0 | reduce | flops 983040 | bytes 4325380 | tf_op jit(solution)/shard_map/reduce_sum | solution.py:20
  132.0 13.3 %all-gather.1 = bf16[64,16,128]{2,1,0:T(8,128)(2,1)S(1)} all-gather(bf16[16,16,128]{2,1,0:T(8,128)(2,1)S(1)} %get-tuple-element.8), channel_id=3, replica_groups=mesh['box_0'=4,'box_1'=2,'dir'=16] {'box_0'}, dimensions={0}, use_global_device_ids=true | all-gather | bytes 327680 | tf_op jit(solution)/shard_map/all_gather | solution.py:31
  145.3 2.2 all_gather.15
  147.5 1.9 all-gather
  149.4 13.4 %all_gather.13 = bf16[8,16,16,128]{3,2,1,0:T(8,128)(2,1)S(1)} all-gather(bf16[2,16,16,128]{3,2,1,0:T(8,128)(2,1)S(1)} %bitcast.103), channel_id=1, replica_groups=mesh['box_0'=4,'box_1'=2,'dir'=16] {'box_0'}, dimensions={0}, use_global_device_ids=true | all-gather | bytes 655360 | tf_op jit(solution)/shard_map/all_gather | solution.py:31
  163.0 0.8 convolution_bitcast_fusion.2
  164.3 1.7 broadcast_in_dim.36
  166.1 5.5 %all-to-all-start.1 = ((bf16[16,32,16,128]{3,2,1,0:T(8,128)(2,1)}), bf16[16,32,16,128]{3,2,1,0:T(8,128)(2,1)S(1)}, u32[]{:S(2)}, u32[]{:S(2)}) async-start(bf16[16,32,16,128]{3,2,1,0:T(8,128)(2,1)} %broadcast_in_dim.36), calls=%async_computation.1 | async-start | bytes 4194304 | tf_op jit(solution)/shard_map/all_to_all | solution.py:58
  171.6 11.5 %convolution_bitcast_fusion.1 = f32[128,256,128]{1,2,0:T(8,128)} fusion(bf16[128,256,128]{2,1,0:T(8,128)(2,1)} %param.10, bf16[3,256,256]{2,1,0:T(8,128)(2,1)S(1)} %copy-done.3), kind=kOutput, calls=%fused_computation.8 | convolution fusion | flops 2147483648 | bytes 25296896 | tf_op jit(solution)/shard_map/pr,lrt->lpt/dot_general | solution.py:149
  183.1 5.8 %convolution_bitcast_fusion = f32[128,256,128]{1,2,0:T(8,128)S(1)} fusion(bf16[128,256,128]{2,1,0:T(8,128)(2,1)} %param.10, bf16[3,256,256]{2,1,0:T(8,128)(2,1)S(1)} %copy-done.3), kind=kOutput, calls=%fused_computation.7 | convolution fusion | flops 2147483648 | bytes 25296896 | tf_op jit(solution)/shard_map/pr,lrt->lpt/dot_general | solution.py:152
  188.9 11.8 %slice.52 = f32[127,256,128]{1,2,0:T(8,128)} slice(f32[128,256,128]{1,2,0:T(8,128)} %convolution_bitcast_fusion.1), slice={[0:127], [0:256], [0:128]} | slice | bytes 33292288 | tf_op jit(solution)/shard_map/slice | solution.py:157
  200.8 6.0 %slice.53 = f32[127,256,128]{1,2,0:T(8,128)} slice(f32[128,256,128]{1,2,0:T(8,128)S(1)} %convolution_bitcast_fusion), slice={[1:128], [0:256], [0:128]} | slice | bytes 33292288 | tf_op jit(solution)/shard_map/slice | solution.py:158
  207.8 1.3 fusion.18
  209.1 11.5 %fusion.4 = f32[2,128,64,256]{3,1,2,0:T(8,128)} fusion(bf16[64,256,256]{2,1,0:T(8,128)(2,1)} %param.19, bf16[2,256,128,1]{2,0,1,3:T(2,128)(2,1)S(1)} %fusion.18), kind=kOutput, calls=%fused_computation.9 | convolution fusion | flops 2147483648 | bytes 25296896 | tf_op jit(solution)/shard_map/spq,bqt->bspt/dot_general | solution.py:141
  220.6 23.8 %fusion.3 = bf16[128,256,128]{1,2,0:T(8,128)(2,1)} fusion(f32[127,256,128]{1,2,0:T(8,128)} %slice.52, f32[1,256,128]{1,2,0:T(8,128)S(1)} %convolution_bitcast_fusion.4, f32[1,256,128]{1,2,0:T(8,128)S(1)} %convolution_bitcast_fusion.3, f32[127,256,128]{1,2,0:T(8,128)} %slice.53, f32[2,128,64,256]{3,1,2,0:T(8,128)} %fusion.4, ...), kind=kOutput, calls=%fused_computation.5 | convolution fusion | flops 2181038080 | bytes 67240960 | tf_op jit(solution)/shard_map/pr,lrt->lpt/dot_general | solution.py:146
  244.4 11.9 %copy.69 = bf16[128,256,128]{2,1,0:T(8,128)(2,1)} copy(bf16[128,256,128]{1,2,0:T(8,128)(2,1)} %fusion.3) | data formatting | bytes 16777216 | tf_op jit(solution)/shard_map/convert_element_type | solution.py:164
  (36 shorter events, 2.2 us)
Async XLA Ops:
  0.0 126.4 %copy-start = (f32[32,64,256]{2,1,0:T(8,128)S(1)}, f32[32,64,256]{2,1,0:T(8,128)}, u32[]{:S(2)}) copy-start(f32[32,64,256]{2,1,0:T(8,128)} %param.17) | copy-start | bytes 6291460
  0.0 8.5 %copy-start.7 = (s32[128]{0:T(128)S(1)}, s32[128]{0:T(128)}, u32[]{:S(2)}) copy-start(s32[128]{0:T(128)} %param.11) | copy-start | bytes 1540
  8.3 20.7 %copy-start.4 = (s32[128,2]{0,1:T(2,128)S(1)}, s32[128,2]{0,1:T(2,128)}, u32[]{:S(2)}) copy-start(s32[128,2]{0,1:T(2,128)} %param.12) | copy-start | bytes 3076
  8.3 20.7 %copy-start.2 = (f32[128]{0:T(128)S(1)}, f32[128]{0:T(128)}, u32[]{:S(2)}) copy-start(f32[128]{0:T(128)} %param.18) | copy-start | bytes 1540
  12.7 116.6 %all-to-all-start = ((f32[16,16,32,128]{3,2,1,0:T(8,128)}), f32[16,16,32,128]{3,2,1,0:T(8,128)}, u32[]{:S(2)}, u32[]{:S(2)}) async-start(f32[16,16,32,128]{3,2,1,0:T(8,128)} %bitcast.97), calls=%async_computation | async-start | bytes 8388608 | tf_op jit(solution)/shard_map/all_to_all | solution.py:19
  21.0 185.7 %collective-permute-start = (bf16[1,256,128]{2,1,0:T(8,128)(2,1)S(1)}, bf16[1,256,128]{2,1,0:T(8,128)(2,1)S(1)}, u32[]{:S(2)}, u32[]{:S(2)}) collective-permute-start(bf16[1,256,128]{2,1,0:T(8,128)(2,1)S(1)} %get-tuple-element.6), channel_id=1, source_target_pairs={{0,1},{1,2},{2,3},{3,4},{4,5},{5,6},{6,7},{7,8},{8,9},{9,10},{10,1... | collective-permute-start | bytes 196616 | tf_op jit(solution)/shard_map/ppermute | solution.py:72
  24.4 182.6 %collective-permute-start.1 = (bf16[1,256,128]{2,1,0:T(8,128)(2,1)S(1)}, bf16[1,256,128]{2,1,0:T(8,128)(2,1)S(1)}, u32[]{:S(2)}, u32[]{:S(2)}) collective-permute-start(bf16[1,256,128]{2,1,0:T(8,128)(2,1)S(1)} %get-tuple-element.5), channel_id=1, source_target_pairs={{1,0},{2,1},{3,2},{4,3},{5,4},{6,5},{7,6},{8,7},{9,8},{10,9},{11,1... | collective-permute-start | bytes 196616 | tf_op jit(solution)/shard_map/ppermute | solution.py:75
  29.1 97.2 %copy-start.5 = (s32[32]{0:T(128)S(1)}, s32[32]{0:T(128)}, u32[]{:S(2)}) copy-start(s32[32]{0:T(128)} %param.16) | copy-start | bytes 388
  29.1 97.3 %copy-start.6 = (s32[32,64]{1,0:T(8,128)S(1)}, s32[32,64]{1,0:T(8,128)}, u32[]{:S(2)}) copy-start(s32[32,64]{1,0:T(8,128)} %param.15) | copy-start | bytes 24580
  131.9 39.6 %copy-start.3 = (bf16[3,256,256]{2,1,0:T(8,128)(2,1)S(1)}, bf16[3,256,256]{2,1,0:T(8,128)(2,1)}, u32[]{:S(2)}) copy-start(bf16[3,256,256]{2,1,0:T(8,128)(2,1)} %param.13) | copy-start | bytes 1179652
  166.1 41.1 %all-to-all-start.1 = ((bf16[16,32,16,128]{3,2,1,0:T(8,128)(2,1)}), bf16[16,32,16,128]{3,2,1,0:T(8,128)(2,1)S(1)}, u32[]{:S(2)}, u32[]{:S(2)}) async-start(bf16[16,32,16,128]{3,2,1,0:T(8,128)(2,1)} %broadcast_in_dim.36), calls=%async_computation.1 | async-start | bytes 4194304 | tf_op jit(solution)/shard_map/all_to_all | solution.py:58
  220.6 35.7 %copy-start.1 = (f32[32,64,256]{2,1,0:T(8,128)S(1)}, f32[32,64,256]{2,1,0:T(8,128)}, u32[]{:S(2)}) copy-start(f32[32,64,256]{2,1,0:T(8,128)} %param.17) | copy-start | bytes 6291460
where the time goes:
time: 257 us; the launch traced here: 256 us
  local copies, waits for them, and re-layouts  131 us (51%)
  matrix products  70.7 us (28%)
  blocking collectives  30.8 us (12%)
  starting transfers between devices  20.9 us (8%)
  other arithmetic  2.84 us (1%)
    gather x1, local copies, waits for them, and re-layouts, time_matrix(): kernel[jnp.clip(sample_lag, 0, length - 1)]  97.2 us
    all_gather x4, blocking collectives, all_blocks(): tiles = lax.all_gather(tiles, axes[k], axis=0, tiled=True)  30.8 us
    dot_general x1, matrix products, per_device(): jnp.einsum('pr,lrt->lpt', near_blocks[0], currents, preferred_element_typ...  23.8 us
    convert_element_type x1, local copies, waits for them, and re-layouts, per_device(): return (near_field + far_field).astype(jnp.bfloat16)  11.9 us
    slice x1, local copies, waits for them, and re-layouts, per_device(): before_term = jnp.concatenate([before_rim[None], before_all[:-1]], axis=0)  11.8 us
    dot_general x1, matrix products, per_device(): jnp.einsum('spq,bqt->bspt', map_block, selected, preferred_element_type=j...  11.5 us
    dot_general x1, matrix products, per_device(): jnp.einsum('pr,lrt->lpt', near_blocks[1], currents, preferred_element_typ...  11.5 us
    dot_general x1, matrix products, per_device(): jnp.einsum('sqp,bspt->bqt', map_block, leaf_runs, preferred_element_type=...  8.31 us
  transfers between devices with their start and end apart: 4, of which 0 were waited for; matrix products, arithmetic and copies ran while one was open for 56% of the time, Pallas kernels for 0%

commit v1 on v0

--- a/solution.py
+++ b/solution.py
@@ -28,7 +28,13 @@
 def all_blocks(array, axes, sequence):
     tiles = array[None]
     for k in sequence:
-        tiles = lax.all_gather(tiles, axes[k], axis=0, tiled=True)
+        pair_the_array = lambda in_array, which_axis: jnp.concatenate(
+            lax.all_to_all(
+                jnp.stack([in_array for _ in range(lax.axis_size(which_axis))]), which_axis, 0, 0
+            ),
+            axis=0,
+        )
+        tiles = pair_the_array(tiles, axes[k])
     held = [lax.axis_size(axes[k]) for k in reversed(sequence)]
     tiles = tiles.reshape(*held, *array.shape)
     turned = sorted(range(len(sequence)), key=lambda place: sequence[len(sequence) - 1 - place])

time: 257 us -> 387 us (1.51)
  local copies, waits for them, and re-layouts: 131 us -> 203 us
  waiting for transfers between devices: 0.01 us -> 49.1 us
  starting transfers between devices: 20.9 us -> 45 us
  blocking collectives: 30.8 us -> 7.99 us
  matrix products: 70.7 us -> 75.7 us
    gather x1, local copies, waits for them, and re-layouts: 97.2 us -> 167 us  [time_matrix(): kernel[jnp.clip(sample_lag, 0, length - 1)]]
    all_to_all x1, waiting for transfers between devices: 0.01 us -> 45.1 us  [summed_on_arrival(): lax.all_to_all(tiles, axis, split_axis=0, concat_axis=0, tiled=True)]
    all_gather x4 -> x0, blocking collectives: 30.8 us -> none  [all_blocks(): tiles = lax.all_gather(tiles, axes[k], axis=0, tiled=True)]
    all_to_all x1, starting transfers between devices: 5.51 us -> 19.2 us  [sent_to_all(): lax.all_to_all(jnp.broadcast_to(array[None], (devices, *array.shape)), ax...]
    all_to_all x0 -> x2, starting transfers between devices: none -> 10.2 us  [all_blocks(): lax.all_to_all(jnp.stack([in_array for _ in range(lax.axis_size(which_axi...]
    all_to_all x0 -> x2, blocking collectives: none -> 7.99 us  [all_blocks(): lax.all_to_all(jnp.stack([in_array for _ in range(lax.axis_size(which_axi...]
    all_to_all x0 -> x2, waiting for transfers between devices: none -> 3.92 us  [all_blocks(): lax.all_to_all(jnp.stack([in_array for _ in range(lax.axis_size(which_axi...]
  transfers between devices with their start and end apart: 4 -> 6, of which waited for: 0 -> 2; matrix products, arithmetic and copies ran while one was open for 56% -> 57% of each run, Pallas kernels for 0% -> 0%
where the time goes in v1:
time: 387 us; the launch traced here: 384 us
  local copies, waits for them, and re-layouts  203 us (52%)
  matrix products  75.7 us (20%)
  waiting for transfers between devices  49.1 us (13%)
  starting transfers between devices  45 us (12%)
  blocking collectives  7.99 us (2%)
    gather x1, local copies, waits for them, and re-layouts, time_matrix(): kernel[jnp.clip(sample_lag, 0, length - 1)]  167 us
    all_to_all x1, waiting for transfers between devices, summed_on_arrival(): lax.all_to_all(tiles, axis, split_axis=0, concat_axis=0, tiled=True)  45.1 us
    dot_general x1, matrix products, per_device(): jnp.einsum('pr,lrt->lpt', near_blocks[0], currents, preferred_element_typ...  23.8 us
    all_to_all x1, starting transfers between devices, sent_to_all(): lax.all_to_all(jnp.broadcast_to(array[None], (devices, *array.shape)), ax...  19.2 us
    convert_element_type x1, local copies, waits for them, and re-layouts, per_device(): return (near_field + far_field).astype(jnp.bfloat16)  11.9 us
    slice x1, local copies, waits for them, and re-layouts, per_device(): before_term = jnp.concatenate([before_rim[None], before_all[:-1]], axis=0)  11.9 us
    dot_general x1, matrix products, per_device(): jnp.einsum('spq,bqt->bspt', map_block, selected, preferred_element_type=j...  11.5 us
    dot_general x1, matrix products, per_device(): jnp.einsum('pr,lrt->lpt', near_blocks[1], currents, preferred_element_typ...  11.5 us
  transfers between devices with their start and end apart: 6, of which 2 were waited for; matrix products, arithmetic and copies ran while one was open for 57% of the time, Pallas kernels for 0%

profile of v1, /device:TPU:34, one launch (start us, length us, event | category | flops | bytes accessed | tf_op | source)
XLA Modules:
  0.0 384.1 jit_solution(7514577259045921569)
XLA Ops:
  0.0 8.3 %fusion.12 = f32[2,256,128]{1,2,0:T(8,128)S(1)} fusion(bf16[2,64,256,128]{3,2,1,0:T(8,128)(2,1)} %bitcast.97, bf16[64,256,256]{2,1,0:T(8,128)(2,1)} %param.14), kind=kOutput, calls=%fused_computation.18 | convolution fusion | flops 2147483648 | bytes 17039360 | tf_op jit(solution)/shard_map/sqp,bspt->bqt/dot_general | solution.py:120
  8.7 3.9 %fusion.47 = f32[256,128,32]{1,2,0:T(8,128)} fusion(f32[2,256,128]{2,0,1:T(2,128)S(1)} %copy.47, s32[2]{0:T(128)S(1)} %slice_reduce_fusion), kind=kOutput, calls=%fused_computation.59 | convolution fusion | flops 25165888 | bytes 4456456 | tf_op jit(solution)/shard_map/bc,bqt->qct/dot_general | solution.py:122
  12.6 7.6 %all-to-all-start = ((f32[16,16,32,128]{3,2,1,0:T(8,128)}), f32[16,16,32,128]{3,2,1,0:T(8,128)}, u32[]{:S(2)}, u32[]{:S(2)}) async-start(f32[16,16,32,128]{3,2,1,0:T(8,128)} %bitcast.98), calls=%async_computation | async-start | bytes 8388608 | tf_op jit(solution)/shard_map/all_to_all | solution.py:19
  21.8 3.4 collective-permute-start
  25.2 4.6 %collective-permute-start.1 = (bf16[1,256,128]{2,1,0:T(8,128)(2,1)}, bf16[1,256,128]{2,1,0:T(8,128)(2,1)}, u32[]{:S(2)}, u32[]{:S(2)}) collective-permute-start(bf16[1,256,128]{2,1,0:T(8,128)(2,1)} %get-tuple-element.5), channel_id=1, source_target_pairs={{1,0},{2,1},{3,2},{4,3},{5,4},{6,5},{7,6},{8,7},{9,8},{10,9},{11,1... | collective-permute-start | bytes 196616 | tf_op jit(solution)/shard_map/ppermute | solution.py:81
  29.8 45.1 %all-to-all-done = f32[16,16,32,128]{3,2,1,0:T(8,128)} async-done(((f32[16,16,32,128]{3,2,1,0:T(8,128)}), f32[16,16,32,128]{3,2,1,0:T(8,128)}, u32[]{:S(2)}, u32[]{:S(2)}) %all-to-all-start) | async-done | bytes 4194336 | tf_op jit(solution)/shard_map/all_to_all | solution.py:19
  74.9 2.6 reduce_sum.9
  77.6 3.8 all_to_all.30
  82.2 5.4 %all-to-all-start.3 = ((bf16[4,1,16,16,128]{4,3,2,1,0:T(8,128)(2,1)}), bf16[4,1,16,16,128]{4,3,2,1,0:T(8,128)(2,1)S(1)}, u32[]{:S(2)}, u32[]{:S(2)}) async-start(bf16[4,1,16,16,128]{4,3,2,1,0:T(8,128)(2,1)} %stack.14), calls=%async_computation.3 | async-start | bytes 524288 | tf_op jit(solution)/shard_map/all_to_all | solution.py:32
  87.7 167.4 %gather_fusion = f32[16384]{0:T(1024)} fusion(f32[128]{0:T(128)S(1)} %copy-done.2, s32[16384]{0:T(1024)S(1)} %fusion.39), kind=kCustom, calls=%fused_computation | custom fusion | bytes 196608 | tf_op jit(solution)/shard_map/gather | solution.py:90
  255.2 4.2 %all_to_all.31 = bf16[2,4,16,16,128]{4,3,1,2,0:T(8,128)(2,1)S(1)} all-to-all(bf16[2,4,16,16,128]{4,3,1,2,0:T(8,128)(2,1)S(1)} %copy.50), channel_id=1, replica_groups=mesh['box_0'=4,'box_1'=2,'dir'=16] {'box_1'}, dimensions={0} | all-to-all | bytes 1048576 | tf_op jit(solution)/shard_map/all_to_all | solution.py:32
  260.2 4.8 %all-to-all-start.2 = ((bf16[4,2,16,16,128]{4,3,1,2,0:T(8,128)(2,1)}), bf16[4,2,16,16,128]{4,3,1,2,0:T(8,128)(2,1)S(1)}, u32[]{:S(2)}, u32[]{:S(2)}) async-start(bf16[4,2,16,16,128]{4,3,1,2,0:T(8,128)(2,1)} %stack.13), calls=%async_computation.2 | async-start | bytes 1048576 | tf_op jit(solution)/shard_map/all_to_all | solution.py:32
  265.1 4.3 %fusion.10 = f32[32,256,16]{1,2,0:T(8,128)} fusion(f32[32,64,256]{2,1,0:T(8,128)S(1)} %copy-done, s32[]{:T(128)S(6)} %select_n.17, f32[32,64]{1,0:T(8,128)S(1)} %fusion.45, s32[32,64]{1,0:T(8,128)} %param.15), kind=kOutput, calls=%fused_computation.15 | convolution fusion | flops 101711872 | bytes 1597444 | tf_op jit(solution)/shard_map/cfs,cfq->csq/dot_general | solution.py:130
  269.4 3.9 %all-to-all-done.2 = bf16[4,2,16,16,128]{4,3,1,2,0:T(8,128)(2,1)S(1)} async-done(((bf16[4,2,16,16,128]{4,3,1,2,0:T(8,128)(2,1)}), bf16[4,2,16,16,128]{4,3,1,2,0:T(8,128)(2,1)S(1)}, u32[]{:S(2)}, u32[]{:S(2)}) %all-to-all-start.2) | async-done | bytes 524320 | tf_op jit(solution)/shard_map/all_to_all | solution.py:32
  273.5 1.8 convolution_bitcast_fusion.2
  276.7 1.7 broadcast_in_dim.13
  278.4 19.2 %all-to-all-start.5 = ((bf16[16,32,16,128]{3,2,1,0:T(8,128)(2,1)}), bf16[16,32,16,128]{3,2,1,0:T(8,128)(2,1)S(1)}, u32[]{:S(2)}, u32[]{:S(2)}) async-start(bf16[16,32,16,128]{3,2,1,0:T(8,128)(2,1)} %broadcast_in_dim.13), calls=%async_computation.5 | async-start | bytes 4194304 | tf_op jit(solution)/shard_map/all_to_all | solution.py:64
  297.6 11.5 %convolution_bitcast_fusion.1 = f32[128,256,128]{1,2,0:T(8,128)} fusion(bf16[128,256,128]{2,1,0:T(8,128)(2,1)} %param.10, bf16[3,256,256]{2,1,0:T(8,128)(2,1)S(1)} %copy-done.3), kind=kOutput, calls=%fused_computation.8 | convolution fusion | flops 2147483648 | bytes 25296896 | tf_op jit(solution)/shard_map/pr,lrt->lpt/dot_general | solution.py:155
  309.1 5.8 %convolution_bitcast_fusion = f32[128,256,128]{1,2,0:T(8,128)S(1)} fusion(bf16[128,256,128]{2,1,0:T(8,128)(2,1)} %param.10, bf16[3,256,256]{2,1,0:T(8,128)(2,1)S(1)} %copy-done.3), kind=kOutput, calls=%fused_computation.7 | convolution fusion | flops 2147483648 | bytes 25296896 | tf_op jit(solution)/shard_map/pr,lrt->lpt/dot_general | solution.py:158
  314.9 11.9 %slice.52 = f32[127,256,128]{1,2,0:T(8,128)} slice(f32[128,256,128]{1,2,0:T(8,128)} %convolution_bitcast_fusion.1), slice={[0:127], [0:256], [0:128]} | slice | bytes 33292288 | tf_op jit(solution)/shard_map/slice | solution.py:163
  326.8 6.0 %slice.53 = f32[127,256,128]{1,2,0:T(8,128)} slice(f32[128,256,128]{1,2,0:T(8,128)S(1)} %convolution_bitcast_fusion), slice={[1:128], [0:256], [0:128]} | slice | bytes 33292288 | tf_op jit(solution)/shard_map/slice | solution.py:164
  336.9 11.5 %fusion.4 = f32[2,128,64,256]{3,1,2,0:T(8,128)} fusion(bf16[64,256,256]{2,1,0:T(8,128)(2,1)} %param.19, bf16[2,256,128,1]{2,0,1,3:T(2,128)(2,1)S(1)} %fusion.18), kind=kOutput, calls=%fused_computation.9 | convolution fusion | flops 2147483648 | bytes 25296896 | tf_op jit(solution)/shard_map/spq,bqt->bspt/dot_general | solution.py:147
  348.4 23.8 %fusion.3 = bf16[128,256,128]{1,2,0:T(8,128)(2,1)} fusion(f32[127,256,128]{1,2,0:T(8,128)} %slice.52, f32[1,256,128]{1,2,0:T(8,128)S(1)} %convolution_bitcast_fusion.4, f32[1,256,128]{1,2,0:T(8,128)S(1)} %convolution_bitcast_fusion.3, f32[127,256,128]{1,2,0:T(8,128)} %slice.53, f32[2,128,64,256]{3,1,2,0:T(8,128)} %fusion.4, ...), kind=kOutput, calls=%fused_computation.5 | convolution fusion | flops 2181038080 | bytes 67240960 | tf_op jit(solution)/shard_map/pr,lrt->lpt/dot_general | solution.py:152
  372.2 11.9 %copy.58 = bf16[128,256,128]{2,1,0:T(8,128)(2,1)} copy(bf16[128,256,128]{1,2,0:T(8,128)(2,1)} %fusion.3) | data formatting | bytes 16777216 | tf_op jit(solution)/shard_map/convert_element_type | solution.py:170
  (42 shorter events, 9.2 us)
Async XLA Ops:
  0.0 265.1 %copy-start = (f32[32,64,256]{2,1,0:T(8,128)S(1)}, f32[32,64,256]{2,1,0:T(8,128)}, u32[]{:S(2)}) copy-start(f32[32,64,256]{2,1,0:T(8,128)} %param.17) | copy-start | bytes 6291460
  0.0 8.5 %copy-start.6 = (s32[128]{0:T(128)S(1)}, s32[128]{0:T(128)}, u32[]{:S(2)}) copy-start(s32[128]{0:T(128)} %param.11) | copy-start | bytes 1540
  8.3 21.4 %copy-start.4 = (s32[128,2]{0,1:T(2,128)S(1)}, s32[128,2]{0,1:T(2,128)}, u32[]{:S(2)}) copy-start(s32[128,2]{0,1:T(2,128)} %param.12) | copy-start | bytes 3076
  12.6 75.0 %copy-start.2 = (f32[128]{0:T(128)S(1)}, f32[128]{0:T(128)}, u32[]{:S(2)}) copy-start(f32[128]{0:T(128)} %param.18) | copy-start | bytes 1540
  12.6 62.3 %all-to-all-start = ((f32[16,16,32,128]{3,2,1,0:T(8,128)}), f32[16,16,32,128]{3,2,1,0:T(8,128)}, u32[]{:S(2)}, u32[]{:S(2)}) async-start(f32[16,16,32,128]{3,2,1,0:T(8,128)} %bitcast.98), calls=%async_computation | async-start | bytes 8388608 | tf_op jit(solution)/shard_map/all_to_all | solution.py:19
  21.8 311.1 %collective-permute-start = (bf16[1,256,128]{2,1,0:T(8,128)(2,1)}, bf16[1,256,128]{2,1,0:T(8,128)(2,1)}, u32[]{:S(2)}, u32[]{:S(2)}) collective-permute-start(bf16[1,256,128]{2,1,0:T(8,128)(2,1)} %get-tuple-element.6), channel_id=1, source_target_pairs={{0,1},{1,2},{2,3},{3,4},{4,5},{5,6},{6,7},{7,8},{8,9},{9,10},{10,1... | collective-permute-start | bytes 196616 | tf_op jit(solution)/shard_map/ppermute | solution.py:78
  25.2 308.8 %collective-permute-start.1 = (bf16[1,256,128]{2,1,0:T(8,128)(2,1)}, bf16[1,256,128]{2,1,0:T(8,128)(2,1)}, u32[]{:S(2)}, u32[]{:S(2)}) collective-permute-start(bf16[1,256,128]{2,1,0:T(8,128)(2,1)} %get-tuple-element.5), channel_id=1, source_target_pairs={{1,0},{2,1},{3,2},{4,3},{5,4},{6,5},{7,6},{8,7},{9,8},{10,9},{11,1... | collective-permute-start | bytes 196616 | tf_op jit(solution)/shard_map/ppermute | solution.py:81
  82.2 172.9 %all-to-all-start.3 = ((bf16[4,1,16,16,128]{4,3,2,1,0:T(8,128)(2,1)}), bf16[4,1,16,16,128]{4,3,2,1,0:T(8,128)(2,1)S(1)}, u32[]{:S(2)}, u32[]{:S(2)}) async-start(bf16[4,1,16,16,128]{4,3,2,1,0:T(8,128)(2,1)} %stack.14), calls=%async_computation.3 | async-start | bytes 524288 | tf_op jit(solution)/shard_map/all_to_all | solution.py:32
  87.6 177.4 %copy-start.5 = (s32[32]{0:T(128)S(1)}, s32[32]{0:T(128)}, u32[]{:S(2)}) copy-start(s32[32]{0:T(128)} %param.16) | copy-start | bytes 388
  259.4 38.2 %copy-start.3 = (bf16[3,256,256]{2,1,0:T(8,128)(2,1)S(1)}, bf16[3,256,256]{2,1,0:T(8,128)(2,1)}, u32[]{:S(2)}) copy-start(bf16[3,256,256]{2,1,0:T(8,128)(2,1)} %param.13) | copy-start | bytes 1179652
  260.2 13.1 %all-to-all-start.2 = ((bf16[4,2,16,16,128]{4,3,1,2,0:T(8,128)(2,1)}), bf16[4,2,16,16,128]{4,3,1,2,0:T(8,128)(2,1)S(1)}, u32[]{:S(2)}, u32[]{:S(2)}) async-start(bf16[4,2,16,16,128]{4,3,1,2,0:T(8,128)(2,1)} %stack.13), calls=%async_computation.2 | async-start | bytes 1048576 | tf_op jit(solution)/shard_map/all_to_all | solution.py:32
  278.4 56.6 %all-to-all-start.5 = ((bf16[16,32,16,128]{3,2,1,0:T(8,128)(2,1)}), bf16[16,32,16,128]{3,2,1,0:T(8,128)(2,1)S(1)}, u32[]{:S(2)}, u32[]{:S(2)}) async-start(bf16[16,32,16,128]{3,2,1,0:T(8,128)(2,1)} %broadcast_in_dim.13), calls=%async_computation.5 | async-start | bytes 4194304 | tf_op jit(solution)/shard_map/all_to_all | solution.py:64
  348.4 35.7 %copy-start.1 = (f32[32,64,256]{2,1,0:T(8,128)S(1)}, f32[32,64,256]{2,1,0:T(8,128)}, u32[]{:S(2)}) copy-start(f32[32,64,256]{2,1,0:T(8,128)} %param.17) | copy-start | bytes 6291460
